TPU v7x, 32 devices: a whole 2x2x4 slice. The times are simulated.
32 devices in a mesh: group: 2 (over y), section: 4 (over z), dp: 4 (over x, core).
Axes of the slice: x: 2, y: 2, z: 4, core: 2. Of those that a mesh axis runs over, the one named last changes fastest.
Arguments:
- tokens: bfloat16 [4, 8, 32, 1600], P(None, ('group', 'dp')), parts along dimension 1, may hold values from -6 to 6
- pixel_index: int32 [4, 8, 384], P(None, ('group', 'dp')), parts along dimension 1, may hold values from 0 to 6271
- point_mask: int32 [4, 8, 384], P(None, ('group', 'dp')), parts along dimension 1, may hold values from 0 to 1, as said below
- point_depth: float32 [4, 8, 384], P(None, ('group', 'dp')), parts along dimension 1, may hold values from -6 to 6
- hook_section: int32 [4], replicated, may hold values from 0 to 2, as said below
- w_query: bfloat16 [4, 1600, 832], P('section')
- w_key: bfloat16 [4, 1600, 832], P('section')
- w_value: bfloat16 [4, 1600, 832], P('section'), may hold values from -0.15625 to 0.15625
- w_output: bfloat16 [4, 832, 1600], P('section'), may hold values from -0.21875 to 0.21875
- reassemble: bfloat16 [5, 1600, 128], P(None, None, ('section', 'dp')), may hold values from -0.15625 to 0.15625
- merging: bfloat16 [4, 128, 128], P(None, None, ('section', 'dp')), may hold values from -0.5 to 0.5
- predict: bfloat16 [128, 196], P(('section', 'dp')), may hold values from -0.5 to 0.5
Outputs:
- grad_query: bfloat16 [8, 1600, 832], P(('group', 'section'), 'dp'), parts along dimension 0
- grad_key: bfloat16 [8, 1600, 832], P(('group', 'section'), 'dp'), parts along dimension 0
- grad_value: bfloat16 [8, 1600, 832], P(('group', 'section'), 'dp'), parts along dimension 0
- grad_output: bfloat16 [8, 832, 1600], P(('group', 'section'), 'dp'), parts along dimension 0
- grad_reassemble: float32 [10, 1600, 128], P('group', None, ('section', 'dp')), parts along dimension 0
- grad_merging: float32 [8, 128, 128], P('group', None, ('section', 'dp')), parts along dimension 0
- grad_predict: float32 [256, 196], P(('group', 'section', 'dp')), parts along dimension 0
There are 2 independent parts, one for each index of `group`. A program takes and returns all parts, laid end to end along the dimension named above; an argument that names none is the same for every part. Nothing has to cross between parts.
Inputs may be any that keep to these rules, and one draw needn't show every extreme that they name: `point_mask`: in each image the valid points come first, and at least 48 of them are valid. `hook_section`: Sorted; the last entry is 2.
All inputs are finite; a program needn't handle non-finite values.
Results may differ from a plain program's by a relative error of at most 0.03.
Values may be sent and summed in bfloat16 or wider, within the bound.
A program may use at most 128 MiB of HBM per device.

v0:
```python
import math
import jax
import jax.numpy as jnp
from jax import lax
from jax.sharding import PartitionSpec as P

HEADS = 13
NHOOK = 4
EPS = 1e-06


def passed_along(block, axis, distance):
    devices = range(lax.axis_size(axis))
    route = [(i - distance, i) for i in devices if i - distance in devices]
    return lax.ppermute(block, axis, route)


def broadcast(value, axis, source):
    kept = jnp.where(lax.axis_index(axis) == source, value, 0).astype(value.dtype)
    return lax.psum(kept, axis)


def as_sent(x):
    return jax.tree.map(lambda a: a.astype(jnp.bfloat16) if a.dtype == jnp.float32 else a, x)


def rms_normed(stream):
    widened = stream.astype(jnp.float32)
    inv_root = lax.rsqrt(jnp.mean(widened * widened, axis=-1, keepdims=True) + EPS)
    return (widened * inv_root).astype(jnp.bfloat16)


def attend(query_rows, key_rows, value_rows):
    image_count, token_count, inner_width = query_rows.shape
    head_width = inner_width // HEADS
    shape_heads = (image_count, token_count, HEADS, head_width)
    query_heads = query_rows.astype(jnp.float32).reshape(shape_heads)
    key_heads = key_rows.astype(jnp.float32).reshape(shape_heads)
    value_heads = value_rows.astype(jnp.float32).reshape(shape_heads)
    scores = jnp.einsum("bqhe,bkhe->bhqk", query_heads, key_heads) / math.sqrt(head_width)
    probabilities = jax.nn.softmax(scores, axis=-1).astype(jnp.bfloat16)
    mixed_heads = jnp.einsum("bhqk,bkhe->bqhe", probabilities.astype(jnp.float32), value_heads)
    return mixed_heads.reshape(image_count, token_count, inner_width).astype(jnp.bfloat16)


def attention_layer(stream, layer_query, layer_key, layer_value, layer_output, nudges):
    image_count, token_count, model_width = stream.shape
    normed = rms_normed(stream).reshape(image_count * token_count, model_width)
    query_rows = (
        jnp.dot(normed, layer_query, preferred_element_type=jnp.float32).astype(jnp.bfloat16)
        + nudges[0]
    )
    key_rows = (
        jnp.dot(normed, layer_key, preferred_element_type=jnp.float32).astype(jnp.bfloat16)
        + nudges[1]
    )
    value_rows = (
        jnp.dot(normed, layer_value, preferred_element_type=jnp.float32).astype(jnp.bfloat16)
        + nudges[2]
    )
    inner_width = layer_query.shape[1]
    mixed = attend(
        query_rows.reshape(image_count, token_count, inner_width),
        key_rows.reshape(image_count, token_count, inner_width),
        value_rows.reshape(image_count, token_count, inner_width),
    )
    mixed_rows = mixed.reshape(image_count * token_count, inner_width)
    update = jnp.dot(mixed_rows, layer_output, preferred_element_type=jnp.float32)
    update = update.reshape(image_count, token_count, model_width)
    output_rows = stream.astype(jnp.float32) + update
    return (output_rows, (normed, mixed_rows))


def reassemble_map(features, weight):
    flat_rows = features.reshape(-1, features.shape[-1]).astype(jnp.bfloat16)
    return jnp.dot(flat_rows, weight, preferred_element_type=jnp.float32).astype(jnp.bfloat16)


def head_rest(projected, top_projected, merging, predict, pixel_index, point_mask, point_depth):
    merged = top_projected.astype(jnp.float32)
    for hook_slot in range(len(projected) - 1, -1, -1):
        activated = jax.nn.silu(merged).astype(jnp.bfloat16)
        merged = projected[hook_slot].astype(jnp.float32) + jnp.dot(
            activated, merging[hook_slot], preferred_element_type=jnp.float32
        )
    activated = jax.nn.silu(merged).astype(jnp.bfloat16)
    depth_rows = jnp.dot(activated, predict, preferred_element_type=jnp.float32)
    depth_map = depth_rows.reshape(pixel_index.shape[0], pixel_index.shape[1], -1)
    picked = jnp.take_along_axis(depth_map, pixel_index, axis=2)
    valid_mask = point_mask.astype(jnp.float32)
    valid_count = jnp.sum(valid_mask, axis=2)
    misfit = (picked - point_depth) * valid_mask
    return jnp.sum(jnp.sum(misfit * misfit, axis=2) / valid_count)


def keep_rows(stream):
    return stream


def put_slot(store_array, item_rows, micro_slot, active):
    updated = lax.dynamic_update_index_in_dim(store_array, item_rows, micro_slot, 0)
    return jnp.where(active, updated, store_array)


def contract(left_rows, right_rows):
    return jnp.einsum("mrd,mrh->dh", left_rows, right_rows, preferred_element_type=jnp.float32)


def on_device(
    tokens,
    pixel_index,
    point_mask,
    point_depth,
    hook_section,
    w_query,
    w_key,
    w_value,
    w_output,
    reassemble,
    merging,
    predict,
):
    section_index = lax.axis_index("section")
    section_count = lax.axis_size("section")
    last_section = section_count - 1
    is_last = section_index == last_section
    micro_count = tokens.shape[0]
    token_rows = tokens.shape[1] * tokens.shape[2]
    model_width = tokens.shape[3]
    inner_width = w_query.shape[2]
    layer_query = w_query[0]
    layer_key = w_key[0]
    layer_value = w_value[0]
    layer_output = w_output[0]
    full_reassemble, full_merging, full_predict = (
        lax.all_gather(reassemble, ("section", "dp"), axis=2, tiled=True),
        lax.all_gather(merging, ("section", "dp"), axis=2, tiled=True),
        lax.all_gather(predict, ("section", "dp"), axis=0, tiled=True),
    )
    zero_nudges = jnp.zeros((3, token_rows, inner_width), jnp.bfloat16)
    zero_rows = jnp.zeros(tokens.shape[1:], jnp.float32)
    empty_store = jnp.zeros(tokens.shape, jnp.float32)

    def run_layer(stream):
        return attention_layer(
            stream, layer_query, layer_key, layer_value, layer_output, zero_nudges
        )[0]

    def forward_step(time_step, carried):
        incoming, inputs_store, outputs_store = carried
        micro_index = time_step - section_index
        active = jnp.logical_and(micro_index >= 0, micro_index < micro_count)
        micro_slot = jnp.clip(micro_index, 0, micro_count - 1)
        fresh_rows = lax.dynamic_index_in_dim(tokens, micro_slot, 0, keepdims=False).astype(
            jnp.float32
        )
        source = jnp.where(section_index == 0, fresh_rows, incoming)
        result = lax.cond(active, run_layer, keep_rows, source)
        inputs_store = put_slot(inputs_store, source, micro_slot, active)
        outputs_store = put_slot(outputs_store, result, micro_slot, active)
        incoming = passed_along(result, "section", 1)
        return (incoming, inputs_store, outputs_store)

    unused, inputs_store, outputs_store = lax.fori_loop(
        0, micro_count + section_count - 1, forward_step, (zero_rows, empty_store, empty_store)
    )
    hook_sum = jnp.zeros(tokens.shape, jnp.float32)
    received = []
    for hook_slot in range(NHOOK):
        local_piece = reassemble_map(outputs_store, full_reassemble[hook_slot])
        received.append(broadcast(local_piece, "section", hook_section[hook_slot]))
    projected_in = tuple(received)

    def head_grads(head_items):

        def loss_terms(projected, top_feature, reassemble_last, head_merging, head_predict):
            top_projected = reassemble_map(top_feature, reassemble_last)
            return head_rest(
                projected,
                top_projected,
                head_merging,
                head_predict,
                pixel_index,
                point_mask,
                point_depth,
            )

        loss_value, pullback = jax.vjp(
            loss_terms,
            head_items[0],
            head_items[1],
            full_reassemble[NHOOK],
            full_merging,
            full_predict,
        )
        return pullback(jnp.ones((), jnp.float32))

    def no_grads(head_items):
        return (
            tuple((jnp.zeros_like(array_item) for array_item in head_items[0])),
            jnp.zeros_like(head_items[1]),
            jnp.zeros_like(full_reassemble[NHOOK]),
            jnp.zeros_like(full_merging),
            jnp.zeros_like(full_predict),
        )

    projected_grads, last_grad, reassemble_last_grad, grad_merging, grad_predict = lax.cond(
        is_last, head_grads, no_grads, (projected_in, outputs_store)
    )
    projected_cotangents = broadcast(jnp.stack(projected_grads), "section", last_section)
    weight_grads = []
    for hook_slot in range(NHOOK):
        unused_rows, pullback = jax.vjp(reassemble_map, outputs_store, full_reassemble[hook_slot])
        feature_grad, weight_grad = pullback(projected_cotangents[hook_slot])
        is_owner = hook_section[hook_slot] == section_index
        hook_sum = hook_sum + jnp.where(is_owner, feature_grad, 0.0)
        weight_grads.append(jnp.where(is_owner, weight_grad, jnp.zeros_like(weight_grad)))
    weight_grads.append(reassemble_last_grad)
    grad_reassemble = jnp.stack(weight_grads)
    hook_grad = hook_sum

    def backward_one(stream, cotangent):

        def local_layer(entry_rows, nudges):
            return attention_layer(
                entry_rows, layer_query, layer_key, layer_value, layer_output, nudges
            )

        unused_rows, pullback, saved = jax.vjp(local_layer, stream, zero_nudges, has_aux=True)
        entry_grad, nudge_grad = pullback(cotangent)
        return (entry_grad, nudge_grad, saved[0], saved[1])

    def skip_one(stream, cotangent):
        return (
            jnp.zeros_like(stream),
            zero_nudges,
            jnp.zeros((token_rows, model_width), jnp.bfloat16),
            jnp.zeros((token_rows, inner_width), jnp.bfloat16),
        )

    def backward_step(time_step, carried):
        incoming, nudge_store, normed_store, mixed_store, cotangent_store = carried
        micro_index = time_step - (last_section - section_index)
        active = jnp.logical_and(micro_index >= 0, micro_index < micro_count)
        micro_slot = jnp.clip(micro_index, 0, micro_count - 1)
        upstream = jnp.where(
            is_last, lax.dynamic_index_in_dim(last_grad, micro_slot, 0, keepdims=False), incoming
        )
        cotangent = upstream + lax.dynamic_index_in_dim(hook_grad, micro_slot, 0, keepdims=False)
        stream = lax.dynamic_index_in_dim(inputs_store, micro_slot, 0, keepdims=False)
        entry_grad, nudge_grad, normed, mixed_rows = lax.cond(
            active, backward_one, skip_one, stream, cotangent
        )
        nudge_store = put_slot(nudge_store, nudge_grad, micro_slot, active)
        normed_store = put_slot(normed_store, normed, micro_slot, active)
        mixed_store = put_slot(mixed_store, mixed_rows, micro_slot, active)
        cotangent_store = put_slot(cotangent_store, cotangent, micro_slot, active)
        incoming = jax.tree.map(
            lambda part, own: part.astype(own.dtype),
            passed_along(as_sent(entry_grad), "section", -1),
            entry_grad,
        )
        return (incoming, nudge_store, normed_store, mixed_store, cotangent_store)

    start_state = (
        zero_rows,
        jnp.zeros((micro_count, 3, token_rows, inner_width), jnp.bfloat16),
        jnp.zeros((micro_count, token_rows, model_width), jnp.bfloat16),
        jnp.zeros((micro_count, token_rows, inner_width), jnp.bfloat16),
        empty_store,
    )
    unused, nudge_store, normed_store, mixed_store, cotangent_store = lax.fori_loop(
        0, micro_count + section_count - 1, backward_step, start_state
    )
    grad_query = contract(normed_store, nudge_store[:, 0])
    grad_key = contract(normed_store, nudge_store[:, 1])
    grad_value = contract(normed_store, nudge_store[:, 2])
    mixed_all = mixed_store.reshape(micro_count * token_rows, inner_width)
    update_grad = cotangent_store.reshape(micro_count * token_rows, model_width)

    def output_map(weight):
        return jnp.dot(mixed_all, weight, preferred_element_type=jnp.float32)

    unused_update, output_pullback = jax.vjp(output_map, layer_output)
    grad_output = output_pullback(update_grad)[0].astype(jnp.float32)
    summed_query, summed_key, summed_value, summed_output = (
        lax.psum_scatter(
            grad_query[None].astype(jnp.bfloat16), "dp", scatter_dimension=1, tiled=True
        ).astype(jnp.float32),
        lax.psum_scatter(
            grad_key[None].astype(jnp.bfloat16), "dp", scatter_dimension=1, tiled=True
        ).astype(jnp.float32),
        lax.psum_scatter(
            grad_value[None].astype(jnp.bfloat16), "dp", scatter_dimension=1, tiled=True
        ).astype(jnp.float32),
        lax.psum_scatter(
            grad_output[None].astype(jnp.bfloat16), "dp", scatter_dimension=1, tiled=True
        ).astype(jnp.float32),
    )
    head_reassemble, head_merging, head_predict = (
        lax.psum_scatter(
            grad_reassemble.astype(jnp.float32), ("section", "dp"), scatter_dimension=2, tiled=True
        ),
        lax.psum_scatter(
            grad_merging.astype(jnp.float32), ("section", "dp"), scatter_dimension=2, tiled=True
        ),
        lax.psum_scatter(
            grad_predict.astype(jnp.float32), ("section", "dp"), scatter_dimension=0, tiled=True
        ),
    )
    return (
        summed_query.astype(jnp.bfloat16),
        summed_key.astype(jnp.bfloat16),
        summed_value.astype(jnp.bfloat16),
        summed_output.astype(jnp.bfloat16),
        head_reassemble,
        head_merging,
        head_predict,
    )


def solution(mesh):
    placed = (
        P(None, ("group", "dp"), None, None),
        P(None, ("group", "dp"), None),
        P(None, ("group", "dp"), None),
        P(None, ("group", "dp"), None),
        P(),
        P("section", None, None),
        P("section", None, None),
        P("section", None, None),
        P("section", None, None),
        P(None, None, ("section", "dp")),
        P(None, None, ("section", "dp")),
        P(("section", "dp"), None),
    )
    return jax.shard_map(
        on_device,
        mesh=mesh,
        in_specs=placed,
        out_specs=(
            P(("group", "section"), "dp", None),
            P(("group", "section"), "dp", None),
            P(("group", "section"), "dp", None),
            P(("group", "section"), "dp", None),
            P("group", None, ("section", "dp")),
            P("group", None, ("section", "dp")),
            P(("group", "section", "dp"), None),
        ),
        check_vma=False,
    )
```

profile of v0, /device:TPU:0, one launch (start us, length us, event | category | flops | bytes accessed | tf_op | source)
XLA Modules:
  0.0 981.0 jit_solution(7728629565180497052)
XLA Ops:
  18.8 5.3 copy.216
  24.1 5.3 copy.214
  30.4 131.4 %while.42 = (s32[]{:T(128)}, f32[1,32,1600]{2,1,0:T(8,128)S(1)}, f32[4,1,32,1600]{3,2,1,0:T(8,128)}, bf16[4,1,32,1600]{3,2,1,0:T(8,128)(2,1)}, s32[]{:T(128)}, /...) while((s32[]{:T(128)}, f32[1,32,1600]{2,1,0:T(8,128)S(1)}, ...), condition=%wide.region_6.7_spmd, body=%wide.region_0.6_spmd.sunk | while | flops 344828992 | bytes 25776712 | solution.py:164
  32.1 10.4 %conditional.7 = (f32[1,32,1600]{2,1,0:T(8,128)S(1)}) conditional(s32[]{:T(128)} %convert_element_type.778, f32[1,32,1600]{2,1,0:T(8,128)S(1)} %get-tuple-element.1149, (f32[1,32,1600]{2,1,0:T(8,128)S(1)}, bf16[1600,832]{1,0:T(8,128)(2,1)}, bf16[1600,832]{1,0:T(8,128)(2,1)S(1)}, bf16[1600,832]{1,0:T(8,128)(2,1)}, bf16[832,1600]{1,0:T(8,128)(2,1)}) %tuple.167), branch_computations={%region_1.1_spmd, %region_2.5_spmd} | conditional | flops 344624192 | bytes 23596836 | solution.py:158
  45.4 7.6 collective-permute-done
  54.7 10.4 %conditional.7 = (f32[1,32,1600]{2,1,0:T(8,128)S(1)}) conditional(s32[]{:T(128)} %convert_element_type.778, f32[1,32,1600]{2,1,0:T(8,128)S(1)} %get-tuple-element.1149, (f32[1,32,1600]{2,1,0:T(8,128)S(1)}, bf16[1600,832]{1,0:T(8,128)(2,1)}, bf16[1600,832]{1,0:T(8,128)(2,1)S(1)}, bf16[1600,832]{1,0:T(8,128)(2,1)}, bf16[832,1600]{1,0:T(8,128)(2,1)}) %tuple.167), branch_computations={%region_1.1_spmd, %region_2.5_spmd} | conditional | flops 344624192 | bytes 23596836 | solution.py:158
  76.0 10.4 %conditional.7 = (f32[1,32,1600]{2,1,0:T(8,128)S(1)}) conditional(s32[]{:T(128)} %convert_element_type.778, f32[1,32,1600]{2,1,0:T(8,128)S(1)} %get-tuple-element.1149, (f32[1,32,1600]{2,1,0:T(8,128)S(1)}, bf16[1600,832]{1,0:T(8,128)(2,1)}, bf16[1600,832]{1,0:T(8,128)(2,1)S(1)}, bf16[1600,832]{1,0:T(8,128)(2,1)}, bf16[832,1600]{1,0:T(8,128)(2,1)}) %tuple.167), branch_computations={%region_1.1_spmd, %region_2.5_spmd} | conditional | flops 344624192 | bytes 23596836 | solution.py:158
  96.4 10.4 %conditional.7 = (f32[1,32,1600]{2,1,0:T(8,128)S(1)}) conditional(s32[]{:T(128)} %convert_element_type.778, f32[1,32,1600]{2,1,0:T(8,128)S(1)} %get-tuple-element.1149, (f32[1,32,1600]{2,1,0:T(8,128)S(1)}, bf16[1600,832]{1,0:T(8,128)(2,1)}, bf16[1600,832]{1,0:T(8,128)(2,1)S(1)}, bf16[1600,832]{1,0:T(8,128)(2,1)}, bf16[832,1600]{1,0:T(8,128)(2,1)}) %tuple.167), branch_computations={%region_1.1_spmd, %region_2.5_spmd} | conditional | flops 344624192 | bytes 23596836 | solution.py:158
  116.2 14.8 %collective-permute-start = (f32[1,32,1600]{2,1,0:T(8,128)S(1)}, f32[1,32,1600]{2,1,0:T(8,128)S(1)}, u32[]{:S(2)}, u32[]{:S(2)}) collective-permute-start(f32[1,32,1600]{2,1,0:T(8,128)S(1)} %get-tuple-element.1302), channel_id=1, source_target_pairs={{0,4},{4,8},{8,12},{1,5},{5,9},{9,13},{2,6},{6,10},{10,14},{3,7},{... | collective-permute-start | bytes 614408 | tf_op jit(solution)/shard_map/while/body/eval_jaxpr/ppermute | solution.py:15
  145.5 12.9 %collective-permute-start = (f32[1,32,1600]{2,1,0:T(8,128)S(1)}, f32[1,32,1600]{2,1,0:T(8,128)S(1)}, u32[]{:S(2)}, u32[]{:S(2)}) collective-permute-start(f32[1,32,1600]{2,1,0:T(8,128)S(1)} %get-tuple-element.1302), channel_id=1, source_target_pairs={{0,4},{4,8},{8,12},{1,5},{5,9},{9,13},{2,6},{6,10},{10,14},{3,7},{... | collective-permute-start | bytes 614408 | tf_op jit(solution)/shard_map/while/body/eval_jaxpr/ppermute | solution.py:15
  170.1 31.5 %all_gather.11 = bf16[128,196]{1,0:T(8,128)(2,1)S(1)} all-gather(bf16[8,196]{1,0:T(8,128)(2,1)S(1)} %copy-done.20), channel_id=1, replica_groups=mesh['group'=2,'section'=4,'dp'=4] {'section','dp'}, dimensions={0}, use_global_device_ids=true | all-gather | bytes 53312 | tf_op jit(solution)/shard_map/all_gather | solution.py:138
  201.6 17.9 %all_gather.10 = bf16[4,128,128]{1,0,2:T(4,128)(2,1)S(1)} all-gather(bf16[4,128,8]{1,0,2:T(4,128)(2,1)S(1)} %copy.217), channel_id=1, replica_groups=mesh['group'=2,'section'=4,'dp'=4] {'section','dp'}, dimensions={2}, use_global_device_ids=true | all-gather | bytes 139264 | tf_op jit(solution)/shard_map/all_gather | solution.py:137
  219.5 4.9 conditional.3
  228.7 75.9 %all-reduce.11.cloned.1.call-done = bf16[4,128,128]{2,1,0:T(8,128)(2,1)} async-done(((bf16[4,128,128]{2,1,0:T(8,128)(2,1)}), bf16[4,128,128]{2,1,0:T(8,128)(2,1)}) %all-reduce.11.cloned.1.call-update) | async-done | bytes 131088 | tf_op jit(solution)/shard_map/psum | solution.py:20
  315.7 278.6 %while.43 = (s32[]{:T(128)}, f32[1,32,1600]{2,1,0:T(8,128)S(1)}, bf16[4,3,32,832]{3,2,0,1:T(8,128)(2,1)}, bf16[4,32,1600]{2,1,0:T(8,128)(2,1)}, bf16[4,32,832]{2...) while((s32[]{:T(128)}, f32[1,32,1600]{2,1,0:T(8,128)S(1)}, ...), condition=%wide.region_24.25_spmd.clone, body=%wide.region_16.24_spmd.clone.sunk | while | flops 608857152 | bytes 61259056 | solution.py:272
  344.9 87.1 %collective-permute-done.1 = bf16[1,32,1600]{2,1,0:T(8,128)(2,1)S(1)} collective-permute-done((bf16[1,32,1600]{2,1,0:T(8,128)(2,1)}, bf16[1,32,1600]{2,1,0:T(8,128)(2,1)S(1)}, u32[]{:S(2)}, u32[]{:S(2)}) %collective-permute-start.1) | collective-permute-done | bytes 102432 | tf_op jit(solution)/shard_map/while/body/eval_jaxpr/ppermute | solution.py:15
  433.8 31.3 %conditional.8 = (bf16[1,32,1600]{2,1,0:T(8,128)(2,1)}, bf16[1,3,32,832]{3,2,1,0:T(8,128)(2,1)S(1)}, bf16[1,32,1600]{2,1,0:T(8,128)(2,1)}, bf16[1,32,832]{2,1,0:T(8,128)(2,1)S(1)}) conditional(s32[]{:T(128)} %convert_element_type.779, () %tuple.170, (f32[1,32,1600]{2,1,0:T(8,128)S(1)}, bf16[832,1600]{1,0:T(8,128)(2,1)}, ...), branch_computations={%region_17.17_spmd, %region_18.23_spmd} | conditional | flops 608443456 | bytes 57541052 | solution.py:251
  474.6 31.3 %conditional.8 = (bf16[1,32,1600]{2,1,0:T(8,128)(2,1)}, bf16[1,3,32,832]{3,2,1,0:T(8,128)(2,1)S(1)}, bf16[1,32,1600]{2,1,0:T(8,128)(2,1)}, bf16[1,32,832]{2,1,0:T(8,128)(2,1)S(1)}) conditional(s32[]{:T(128)} %convert_element_type.779, () %tuple.170, (f32[1,32,1600]{2,1,0:T(8,128)S(1)}, bf16[832,1600]{1,0:T(8,128)(2,1)}, ...), branch_computations={%region_17.17_spmd, %region_18.23_spmd} | conditional | flops 608443456 | bytes 57541052 | solution.py:251
  515.3 31.3 %conditional.8 = (bf16[1,32,1600]{2,1,0:T(8,128)(2,1)}, bf16[1,3,32,832]{3,2,1,0:T(8,128)(2,1)S(1)}, bf16[1,32,1600]{2,1,0:T(8,128)(2,1)}, bf16[1,32,832]{2,1,0:T(8,128)(2,1)S(1)}) conditional(s32[]{:T(128)} %convert_element_type.779, () %tuple.170, (f32[1,32,1600]{2,1,0:T(8,128)S(1)}, bf16[832,1600]{1,0:T(8,128)(2,1)}, ...), branch_computations={%region_17.17_spmd, %region_18.23_spmd} | conditional | flops 608443456 | bytes 57541052 | solution.py:251
  556.0 31.3 %conditional.8 = (bf16[1,32,1600]{2,1,0:T(8,128)(2,1)}, bf16[1,3,32,832]{3,2,1,0:T(8,128)(2,1)S(1)}, bf16[1,32,1600]{2,1,0:T(8,128)(2,1)}, bf16[1,32,832]{2,1,0:T(8,128)(2,1)S(1)}) conditional(s32[]{:T(128)} %convert_element_type.779, () %tuple.170, (f32[1,32,1600]{2,1,0:T(8,128)S(1)}, bf16[832,1600]{1,0:T(8,128)(2,1)}, ...), branch_computations={%region_17.17_spmd, %region_18.23_spmd} | conditional | flops 608443456 | bytes 57541052 | solution.py:251
  596.3 12.4 %copy.242 = bf16[1,1600,832]{2,0,1:T(2,128)(2,1)} copy(bf16[1,1600,832]{1,2,0:T(8,128)(2,1)S(1)} %fusion.92) | data formatting | bytes 5324800
  608.8 4.7 copy.332
  617.2 14.5 %copy.244 = bf16[1,1600,832]{2,0,1:T(2,128)(2,1)} copy(bf16[1,1600,832]{1,2,0:T(8,128)(2,1)} %fusion.93) | data formatting | bytes 5324800
  631.7 4.6 copy.331
  639.1 14.4 %copy.240 = bf16[1,1600,832]{2,0,1:T(2,128)(2,1)} copy(bf16[1,1600,832]{1,2,0:T(8,128)(2,1)} %fusion.91) | data formatting | bytes 5324800
  664.7 4.8 copy.229
  679.4 8.6 reduce-scatter.26.cloned.1.call-done
  690.7 35.9 %reduce-scatter.22.cloned.1.call-done = bf16[400,832]{1,0:T(8,128)(2,1)} async-done(((bf16[1600,832]{1,0:T(8,128)(2,1)}), bf16[400,832]{1,0:T(8,128)(2,1)}) %reduce-scatter.22.cloned.1.call-update) | async-done | bytes 665616
  729.4 90.1 %reduce-scatter.18.cloned.1.call-done = f32[5,1600,8]{1,0,2:T(8,128)} async-done(((f32[5,1600,128]{1,0,2:T(8,128)}), f32[5,1600,8]{1,0,2:T(8,128)}) %reduce-scatter.18.cloned.1.call-update) | async-done | bytes 256016 | tf_op jit(solution)/shard_map/reduce_scatter | solution.py:301
  821.3 56.8 %reduce-scatter.28.cloned.1.call-done = f32[8,196]{1,0:T(8,128)} async-done(((f32[128,196]{1,0:T(8,128)}), f32[8,196]{1,0:T(8,128)}) %reduce-scatter.28.cloned.1.call-update) | async-done | bytes 6288
  878.1 58.5 %reduce-scatter.20.cloned.1.call-done = f32[4,128,8]{1,2,0:T(8,128)} async-done(((f32[4,128,128]{1,2,0:T(8,128)}), f32[4,128,8]{1,2,0:T(8,128)}) %reduce-scatter.20.cloned.1.call-update) | async-done | bytes 16400 | tf_op jit(solution)/shard_map/reduce_scatter | solution.py:304
  936.6 37.6 %reduce-scatter.16.cloned.1.call-done = bf16[1,208,1600]{2,1,0:T(8,128)(2,1)} async-done(((bf16[1,832,1600]{2,1,0:T(8,128)(2,1)}), bf16[1,208,1600]{2,1,0:T(8,128)(2,1)}) %reduce-scatter.16.cloned.1.call-update) | async-done | bytes 665616 | tf_op jit(solution)/shard_map/reduce_scatter | solution.py:296
  (456 shorter events, 362.8 us)
Async XLA Ops:
  7.2 154.6 %all-gather.2.cloned.1.call-start = ((), (), s32[]{:S(2)}) async-start(), calls=%async_computation.7 | async-start | bytes 2263040 | tf_op jit(solution)/shard_map/all_gather | solution.py:136
  7.9 211.6 %all-reduce.13.cloned.1.call-start = ((), (), s32[]{:S(2)}) async-start(), calls=%async_computation.16 | async-start | bytes 262144 | tf_op jit(solution)/shard_map/psum | solution.py:20
  42.5 10.5 %collective-permute-start = (f32[1,32,1600]{2,1,0:T(8,128)S(1)}, f32[1,32,1600]{2,1,0:T(8,128)S(1)}, u32[]{:S(2)}, u32[]{:S(2)}) collective-permute-start(f32[1,32,1600]{2,1,0:T(8,128)S(1)} %get-tuple-element.1302), channel_id=1, source_target_pairs={{0,4},{4,8},{8,12},{1,5},{5,9},{9,13},{2,6},{6,10},{10,14},{3,7},{... | collective-permute-start | bytes 614408 | tf_op jit(solution)/shard_map/while/body/eval_jaxpr/ppermute | solution.py:15
  65.1 9.2 collective-permute-start
  86.4 8.3 collective-permute-start
  106.8 7.7 collective-permute-start
  116.2 18.1 %collective-permute-start = (f32[1,32,1600]{2,1,0:T(8,128)S(1)}, f32[1,32,1600]{2,1,0:T(8,128)S(1)}, u32[]{:S(2)}, u32[]{:S(2)}) collective-permute-start(f32[1,32,1600]{2,1,0:T(8,128)S(1)} %get-tuple-element.1302), channel_id=1, source_target_pairs={{0,4},{4,8},{8,12},{1,5},{5,9},{9,13},{2,6},{6,10},{10,14},{3,7},{... | collective-permute-start | bytes 614408 | tf_op jit(solution)/shard_map/while/body/eval_jaxpr/ppermute | solution.py:15
  136.1 7.7 collective-permute-start
  145.5 16.2 %collective-permute-start = (f32[1,32,1600]{2,1,0:T(8,128)S(1)}, f32[1,32,1600]{2,1,0:T(8,128)S(1)}, u32[]{:S(2)}, u32[]{:S(2)}) collective-permute-start(f32[1,32,1600]{2,1,0:T(8,128)S(1)} %get-tuple-element.1302), channel_id=1, source_target_pairs={{0,4},{4,8},{8,12},{1,5},{5,9},{9,13},{2,6},{6,10},{10,14},{3,7},{... | collective-permute-start | bytes 614408 | tf_op jit(solution)/shard_map/while/body/eval_jaxpr/ppermute | solution.py:15
  161.7 8.3 copy-start.18
  161.7 8.3 copy-start.20
  161.7 57.7 %copy-start.16 = (s32[4,1,384]{2,1,0:T(1,128)S(1)}, s32[4,1,384]{2,1,0:T(1,128)}, u32[]{:S(2)}) copy-start(s32[4,1,384]{2,1,0:T(1,128)} %param.23) | copy-start | bytes 18436
  161.7 57.7 %copy-start.17 = (s32[4,1,384]{2,1,0:T(1,128)S(1)}, s32[4,1,384]{2,1,0:T(1,128)}, u32[]{:S(2)}) copy-start(s32[4,1,384]{2,1,0:T(1,128)} %param.24) | copy-start | bytes 18436
  161.8 57.7 %copy-start.19 = (f32[4,1,384]{2,1,0:T(1,128)S(1)}, f32[4,1,384]{2,1,0:T(1,128)}, u32[]{:S(2)}) copy-start(f32[4,1,384]{2,1,0:T(1,128)} %param.25) | copy-start | bytes 18436
  170.0 134.6 %all-reduce.11.cloned.1.call-start = ((), (), s32[]{:S(2)}) async-start(), calls=%async_computation.8 | async-start | bytes 262144 | tf_op jit(solution)/shard_map/psum | solution.py:20
  226.0 450.6 %reduce-scatter.24.cloned.1.call-start = ((), (), s32[]{:S(2)}) async-start(), calls=%async_computation.13 | async-start | bytes 3584000
  318.8 6.8 collective-permute-start.1
  328.8 6.8 collective-permute-start.1
  338.9 93.1 %collective-permute-start.1 = (bf16[1,32,1600]{2,1,0:T(8,128)(2,1)}, bf16[1,32,1600]{2,1,0:T(8,128)(2,1)S(1)}, u32[]{:S(2)}, u32[]{:S(2)}) collective-permute-start(bf16[1,32,1600]{2,1,0:T(8,128)(2,1)} %get-tuple-element.1167), channel_id=1, source_target_pairs={{4,0},{8,4},{12,8},{5,1},{9,5},{13,9},{6,2},{10,6},{14,10},{7,3},{... | collective-permute-start | bytes 307208 | tf_op jit(solution)/shard_map/while/body/eval_jaxpr/ppermute | solution.py:15
  461.2 3.8 copy-start.7
  465.1 7.6 collective-permute-start.1
  505.9 7.6 collective-permute-start.1
  542.7 3.8 copy-start.7
  546.6 7.6 collective-permute-start.1
  587.3 7.0 collective-permute-start.1
  613.5 74.4 %reduce-scatter.26.cloned.1.call-start = ((), (), s32[]{:S(2)}) async-start(), calls=%async_computation.14 | async-start | bytes 3584000
  636.4 90.3 %reduce-scatter.22.cloned.1.call-start = ((), (), s32[]{:S(2)}) async-start(), calls=%async_computation.12 | async-start | bytes 3584000
  658.1 6.5 copy-start.11
  658.2 161.4 %reduce-scatter.18.cloned.1.call-start = ((), (), s32[]{:S(2)}) async-start(), calls=%async_computation.10 | async-start | bytes 7241728 | tf_op jit(solution)/shard_map/reduce_scatter | solution.py:301
  669.5 208.6 %reduce-scatter.28.cloned.1.call-start = ((), (), s32[]{:S(2)}) async-start(), calls=%async_computation.15 | async-start | bytes 139264
  671.2 265.4 %reduce-scatter.20.cloned.1.call-start = ((), (), s32[]{:S(2)}) async-start(), calls=%async_computation.11 | async-start | bytes 278528 | tf_op jit(solution)/shard_map/reduce_scatter | solution.py:304
  673.0 301.2 %reduce-scatter.16.cloned.1.call-start = ((), (), s32[]{:S(2)}) async-start(), calls=%async_computation.9 | async-start | bytes 3461120 | tf_op jit(solution)/shard_map/reduce_scatter | solution.py:296
  (35 other events, 96.7 us)
Sparse Core Ops, SparseCore 0:
  10.2 44.1 all-gather.1
  170.1 45.8 all-reduce.12
  226.1 78.4 all-reduce.10
  613.6 35.4 reduce-scatter.23
  651.7 36.2 reduce-scatter.25
  690.3 36.2 reduce-scatter.21
  731.1 88.3 reduce-scatter.17
  823.6 54.5 reduce-scatter.27
  882.2 54.3 reduce-scatter.19
  939.6 34.5 reduce-scatter.15
where the time goes:
time: 987 us; the launch traced here: 981 us
  waiting for transfers between devices  475 us (48%)
  matrix products  149 us (15%)
  local copies, waits for them, and re-layouts  142 us (14%)
  other arithmetic  88.3 us (9%)
  starting transfers between devices  56.4 us (6%)
  blocking collectives  49.4 us (5%)
  between operations  19.4 us (2%)
    ppermute x14, waiting for transfers between devices, passed_along(): return lax.ppermute(block, axis, route)  111 us
    unnamed x14, waiting for transfers between devices  102 us
    reduce_scatter x1, waiting for transfers between devices, on_device(): lax.psum_scatter(grad_reassemble.astype(jnp.float32), ('section', 'dp'),...  90.1 us
    unnamed x43, local copies, waits for them, and re-layouts  85.7 us
    psum x2, waiting for transfers between devices, broadcast(): return lax.psum(kept, axis)  75.9 us
    select_n x42, other arithmetic, put_slot(): return jnp.where(active, updated, store_array)  65.6 us
    reduce_scatter x1, waiting for transfers between devices, on_device(): lax.psum_scatter(grad_merging.astype(jnp.float32), ('section', 'dp'), sca...  58.5 us
    ppermute x14, starting transfers between devices, passed_along(): return lax.ppermute(block, axis, route)  55.6 us
  transfers between devices with their start and end apart: 24, of which 20 were waited for; matrix products, arithmetic and copies ran while one was open for 20% of the time, Pallas kernels for 0%

commit v1 on v0

--- a/solution.py
+++ b/solution.py
@@ -17,7 +17,7 @@
 
 def broadcast(value, axis, source):
     kept = jnp.where(lax.axis_index(axis) == source, value, 0).astype(value.dtype)
-    return lax.psum(kept, axis)
+    return jnp.sum(lax.all_gather(kept, axis), axis=0)
 
 
 def as_sent(x):

time: 987 us -> 1030 us (1.044)
  blocking collectives: 49.4 us -> 175 us
  waiting for transfers between devices: 475 us -> 397 us
    all_gather x0 -> x5, blocking collectives: none -> 131 us  [broadcast(): return jnp.sum(lax.all_gather(kept, axis), axis=0)]
    psum x2 -> x0, waiting for transfers between devices: 75.9 us -> none  [broadcast(): return lax.psum(kept, axis)]
    unnamed x14 -> x12, waiting for transfers between devices: 102 us -> 103 us
  transfers between devices with their start and end apart: 24 -> 22, of which waited for: 20 -> 19; matrix products, arithmetic and copies ran while one was open for 20% -> 19% of each run, Pallas kernels for 0% -> 0%
where the time goes in v1:
time: 1030 us
  waiting for transfers between devices  397 us (39%)
  blocking collectives  175 us (17%)
  matrix products  147 us (14%)
  local copies, waits for them, and re-layouts  143 us (14%)
  other arithmetic  87.6 us (9%)
  starting transfers between devices  56.1 us (5%)
  between operations  19.6 us (2%)
    all_gather x5, blocking collectives, broadcast(): return jnp.sum(lax.all_gather(kept, axis), axis=0)  131 us
    ppermute x14, waiting for transfers between devices, passed_along(): return lax.ppermute(block, axis, route)  108 us
    unnamed x12, waiting for transfers between devices  103 us
    reduce_scatter x1, waiting for transfers between devices, on_device(): lax.psum_scatter(grad_reassemble.astype(jnp.float32), ('section', 'dp'),...  90.1 us
    unnamed x43, local copies, waits for them, and re-layouts  87.1 us
    select_n x42, other arithmetic, put_slot(): return jnp.where(active, updated, store_array)  65.6 us
    reduce_scatter x1, waiting for transfers between devices, on_device(): lax.psum_scatter(grad_merging.astype(jnp.float32), ('section', 'dp'), sca...  58.4 us
    ppermute x14, starting transfers between devices, passed_along(): return lax.ppermute(block, axis, route)  55.5 us
  transfers between devices with their start and end apart: 22, of which 19 were waited for; matrix products, arithmetic and copies ran while one was open for 19% of the time, Pallas kernels for 0%

profile of v1, /device:TPU:0, one launch (start us, length us, event | category | flops | bytes accessed | tf_op | source)
XLA Modules:
  0.0 1026.1 jit_solution(6272283539864168442)
XLA Ops:
  16.0 24.9 %all_gather.47 = bf16[128,196]{1,0:T(8,128)(2,1)} all-gather(bf16[8,196]{1,0:T(8,128)(2,1)} %param.33), channel_id=1, replica_groups=mesh['group'=2,'section'=4,'dp'=4] {'section','dp'}, dimensions={0}, use_global_device_ids=true | all-gather | bytes 53312 | tf_op jit(solution)/shard_map/all_gather | solution.py:138
  40.9 19.3 %all_gather.46 = bf16[4,128,128]{1,0,2:T(4,128)(2,1)} all-gather(bf16[4,128,8]{1,0,2:T(4,128)(2,1)S(1)} %copy.217), channel_id=1, replica_groups=mesh['group'=2,'section'=4,'dp'=4] {'section','dp'}, dimensions={2}, use_global_device_ids=true | all-gather | bytes 139264 | tf_op jit(solution)/shard_map/all_gather | solution.py:137
  66.2 5.3 copy.216
  71.5 5.3 copy.214
  77.8 126.7 %while.42 = (s32[]{:T(128)}, f32[1,32,1600]{2,1,0:T(8,128)S(1)}, f32[4,1,32,1600]{3,2,1,0:T(8,128)}, bf16[4,1,32,1600]{3,2,1,0:T(8,128)(2,1)}, s32[]{:T(128)}, /...) while((s32[]{:T(128)}, f32[1,32,1600]{2,1,0:T(8,128)S(1)}, ...), condition=%wide.region_6.7_spmd, body=%wide.region_0.6_spmd.sunk | while | flops 344828992 | bytes 25776712 | solution.py:164
  79.5 10.4 %conditional.7 = (f32[1,32,1600]{2,1,0:T(8,128)S(1)}) conditional(s32[]{:T(128)} %convert_element_type.825, f32[1,32,1600]{2,1,0:T(8,128)S(1)} %get-tuple-element.1180, (f32[1,32,1600]{2,1,0:T(8,128)S(1)}, bf16[1600,832]{1,0:T(8,128)(2,1)}, bf16[1600,832]{1,0:T(8,128)(2,1)S(1)}, bf16[1600,832]{1,0:T(8,128)(2,1)}, bf16[832,1600]{1,0:T(8,128)(2,1)}) %tuple.169), branch_computations={%region_1.1_spmd, %region_2.5_spmd} | conditional | flops 344624192 | bytes 23596836 | solution.py:158
  98.1 10.4 %conditional.7 = (f32[1,32,1600]{2,1,0:T(8,128)S(1)}) conditional(s32[]{:T(128)} %convert_element_type.825, f32[1,32,1600]{2,1,0:T(8,128)S(1)} %get-tuple-element.1180, (f32[1,32,1600]{2,1,0:T(8,128)S(1)}, bf16[1600,832]{1,0:T(8,128)(2,1)}, bf16[1600,832]{1,0:T(8,128)(2,1)S(1)}, bf16[1600,832]{1,0:T(8,128)(2,1)}, bf16[832,1600]{1,0:T(8,128)(2,1)}) %tuple.169), branch_computations={%region_1.1_spmd, %region_2.5_spmd} | conditional | flops 344624192 | bytes 23596836 | solution.py:158
  119.1 10.4 %conditional.7 = (f32[1,32,1600]{2,1,0:T(8,128)S(1)}) conditional(s32[]{:T(128)} %convert_element_type.825, f32[1,32,1600]{2,1,0:T(8,128)S(1)} %get-tuple-element.1180, (f32[1,32,1600]{2,1,0:T(8,128)S(1)}, bf16[1600,832]{1,0:T(8,128)(2,1)}, bf16[1600,832]{1,0:T(8,128)(2,1)S(1)}, bf16[1600,832]{1,0:T(8,128)(2,1)}, bf16[832,1600]{1,0:T(8,128)(2,1)}) %tuple.169), branch_computations={%region_1.1_spmd, %region_2.5_spmd} | conditional | flops 344624192 | bytes 23596836 | solution.py:158
  139.1 10.4 %conditional.7 = (f32[1,32,1600]{2,1,0:T(8,128)S(1)}) conditional(s32[]{:T(128)} %convert_element_type.825, f32[1,32,1600]{2,1,0:T(8,128)S(1)} %get-tuple-element.1180, (f32[1,32,1600]{2,1,0:T(8,128)S(1)}, bf16[1600,832]{1,0:T(8,128)(2,1)}, bf16[1600,832]{1,0:T(8,128)(2,1)S(1)}, bf16[1600,832]{1,0:T(8,128)(2,1)}, bf16[832,1600]{1,0:T(8,128)(2,1)}) %tuple.169), branch_computations={%region_1.1_spmd, %region_2.5_spmd} | conditional | flops 344624192 | bytes 23596836 | solution.py:158
  158.9 14.8 %collective-permute-start = (f32[1,32,1600]{2,1,0:T(8,128)S(1)}, f32[1,32,1600]{2,1,0:T(8,128)S(1)}, u32[]{:S(2)}, u32[]{:S(2)}) collective-permute-start(f32[1,32,1600]{2,1,0:T(8,128)S(1)} %get-tuple-element.1329), channel_id=1, source_target_pairs={{0,4},{4,8},{8,12},{1,5},{5,9},{9,13},{2,6},{6,10},{10,14},{3,7},{... | collective-permute-start | bytes 614408 | tf_op jit(solution)/shard_map/while/body/eval_jaxpr/ppermute | solution.py:15
  188.2 12.9 %collective-permute-start = (f32[1,32,1600]{2,1,0:T(8,128)S(1)}, f32[1,32,1600]{2,1,0:T(8,128)S(1)}, u32[]{:S(2)}, u32[]{:S(2)}) collective-permute-start(f32[1,32,1600]{2,1,0:T(8,128)S(1)} %get-tuple-element.1329), channel_id=1, source_target_pairs={{0,4},{4,8},{8,12},{1,5},{5,9},{9,13},{2,6},{6,10},{10,14},{3,7},{... | collective-permute-start | bytes 614408 | tf_op jit(solution)/shard_map/while/body/eval_jaxpr/ppermute | solution.py:15
  205.9 24.5 %all-gather = bf16[512,128]{1,0:T(8,128)(2,1)S(1)} all-gather(bf16[128,128]{1,0:T(8,128)(2,1)S(1)} %fusion.117), channel_id=2, replica_groups=mesh['group'=2,'section'=4,'dp'=4] {'section'}, dimensions={0}, use_global_device_ids=true | all-gather | bytes 163840 | tf_op jit(solution)/shard_map/all_gather | solution.py:20
  231.8 14.2 %all-gather.1 = bf16[512,128]{1,0:T(8,128)(2,1)} all-gather(bf16[128,128]{1,0:T(8,128)(2,1)S(1)} %fusion.118), channel_id=3, replica_groups=mesh['group'=2,'section'=4,'dp'=4] {'section'}, dimensions={0}, use_global_device_ids=true | all-gather | bytes 163840 | tf_op jit(solution)/shard_map/all_gather | solution.py:20
  247.4 14.2 %all-gather.2 = bf16[512,128]{1,0:T(8,128)(2,1)} all-gather(bf16[128,128]{1,0:T(8,128)(2,1)S(1)} %fusion.119), channel_id=4, replica_groups=mesh['group'=2,'section'=4,'dp'=4] {'section'}, dimensions={0}, use_global_device_ids=true | all-gather | bytes 163840 | tf_op jit(solution)/shard_map/all_gather | solution.py:20
  263.1 14.3 %all-gather.3 = bf16[512,128]{1,0:T(8,128)(2,1)} all-gather(bf16[128,128]{1,0:T(8,128)(2,1)S(1)} %fusion.120), channel_id=5, replica_groups=mesh['group'=2,'section'=4,'dp'=4] {'section'}, dimensions={0}, use_global_device_ids=true | all-gather | bytes 163840 | tf_op jit(solution)/shard_map/all_gather | solution.py:20
  277.3 4.9 conditional.3
  283.8 63.6 %all_gather.48 = bf16[4,4,128,128]{3,2,1,0:T(8,128)(2,1)S(1)} all-gather(bf16[1,4,128,128]{3,2,1,0:T(8,128)(2,1)S(1)} %maximum_select_fusion), channel_id=1, replica_groups=mesh['group'=2,'section'=4,'dp'=4] {'section'}, dimensions={0}, use_global_device_ids=true | all-gather | bytes 655360 | tf_op jit(solution)/shard_map/all_gather | solution.py:20
  358.6 280.3 %while.43 = (s32[]{:T(128)}, f32[1,32,1600]{2,1,0:T(8,128)S(1)}, bf16[4,3,32,832]{3,2,0,1:T(8,128)(2,1)}, bf16[4,32,1600]{2,1,0:T(8,128)(2,1)}, bf16[4,32,832]{2...) while((s32[]{:T(128)}, f32[1,32,1600]{2,1,0:T(8,128)S(1)}, ...), condition=%wide.region_24.25_spmd.clone, body=%wide.region_16.24_spmd.clone.sunk | while | flops 608857152 | bytes 61259056 | solution.py:272
  387.8 88.9 %collective-permute-done.1 = bf16[1,32,1600]{2,1,0:T(8,128)(2,1)S(1)} collective-permute-done((bf16[1,32,1600]{2,1,0:T(8,128)(2,1)}, bf16[1,32,1600]{2,1,0:T(8,128)(2,1)S(1)}, u32[]{:S(2)}, u32[]{:S(2)}) %collective-permute-start.1) | collective-permute-done | bytes 102432 | tf_op jit(solution)/shard_map/while/body/eval_jaxpr/ppermute | solution.py:15
  478.6 31.3 %conditional.8 = (bf16[1,32,1600]{2,1,0:T(8,128)(2,1)}, bf16[1,3,32,832]{3,2,1,0:T(8,128)(2,1)S(1)}, bf16[1,32,1600]{2,1,0:T(8,128)(2,1)}, bf16[1,32,832]{2,1,0:T(8,128)(2,1)S(1)}) conditional(s32[]{:T(128)} %convert_element_type.826, () %tuple.172, (f32[1,32,1600]{2,1,0:T(8,128)S(1)}, bf16[832,1600]{1,0:T(8,128)(2,1)}, ...), branch_computations={%region_17.17_spmd, %region_18.23_spmd} | conditional | flops 608443456 | bytes 57541052 | solution.py:251
  519.3 31.3 %conditional.8 = (bf16[1,32,1600]{2,1,0:T(8,128)(2,1)}, bf16[1,3,32,832]{3,2,1,0:T(8,128)(2,1)S(1)}, bf16[1,32,1600]{2,1,0:T(8,128)(2,1)}, bf16[1,32,832]{2,1,0:T(8,128)(2,1)S(1)}) conditional(s32[]{:T(128)} %convert_element_type.826, () %tuple.172, (f32[1,32,1600]{2,1,0:T(8,128)S(1)}, bf16[832,1600]{1,0:T(8,128)(2,1)}, ...), branch_computations={%region_17.17_spmd, %region_18.23_spmd} | conditional | flops 608443456 | bytes 57541052 | solution.py:251
  560.0 31.3 %conditional.8 = (bf16[1,32,1600]{2,1,0:T(8,128)(2,1)}, bf16[1,3,32,832]{3,2,1,0:T(8,128)(2,1)S(1)}, bf16[1,32,1600]{2,1,0:T(8,128)(2,1)}, bf16[1,32,832]{2,1,0:T(8,128)(2,1)S(1)}) conditional(s32[]{:T(128)} %convert_element_type.826, () %tuple.172, (f32[1,32,1600]{2,1,0:T(8,128)S(1)}, bf16[832,1600]{1,0:T(8,128)(2,1)}, ...), branch_computations={%region_17.17_spmd, %region_18.23_spmd} | conditional | flops 608443456 | bytes 57541052 | solution.py:251
  600.7 31.3 %conditional.8 = (bf16[1,32,1600]{2,1,0:T(8,128)(2,1)}, bf16[1,3,32,832]{3,2,1,0:T(8,128)(2,1)S(1)}, bf16[1,32,1600]{2,1,0:T(8,128)(2,1)}, bf16[1,32,832]{2,1,0:T(8,128)(2,1)S(1)}) conditional(s32[]{:T(128)} %convert_element_type.826, () %tuple.172, (f32[1,32,1600]{2,1,0:T(8,128)S(1)}, bf16[832,1600]{1,0:T(8,128)(2,1)}, ...), branch_computations={%region_17.17_spmd, %region_18.23_spmd} | conditional | flops 608443456 | bytes 57541052 | solution.py:251
  641.0 12.4 %copy.242 = bf16[1,1600,832]{2,0,1:T(2,128)(2,1)} copy(bf16[1,1600,832]{1,2,0:T(8,128)(2,1)S(1)} %fusion.92) | data formatting | bytes 5324800
  661.7 14.5 %copy.244 = bf16[1,1600,832]{2,0,1:T(2,128)(2,1)} copy(bf16[1,1600,832]{1,2,0:T(8,128)(2,1)} %fusion.93) | data formatting | bytes 5324800
  683.6 14.3 %copy.240 = bf16[1,1600,832]{2,0,1:T(2,128)(2,1)} copy(bf16[1,1600,832]{1,2,0:T(8,128)(2,1)} %fusion.91) | data formatting | bytes 5324800
  723.9 9.3 reduce-scatter.26.cloned.1.call-done
  736.0 35.9 %reduce-scatter.22.cloned.1.call-done = bf16[400,832]{1,0:T(8,128)(2,1)} async-done(((bf16[1600,832]{1,0:T(8,128)(2,1)}), bf16[400,832]{1,0:T(8,128)(2,1)}) %reduce-scatter.22.cloned.1.call-update) | async-done | bytes 665616
  774.7 90.1 %reduce-scatter.18.cloned.1.call-done = f32[5,1600,8]{1,0,2:T(8,128)} async-done(((f32[5,1600,128]{1,0,2:T(8,128)}), f32[5,1600,8]{1,0,2:T(8,128)}) %reduce-scatter.18.cloned.1.call-update) | async-done | bytes 256016 | tf_op jit(solution)/shard_map/reduce_scatter | solution.py:301
  866.5 56.6 %reduce-scatter.28.cloned.1.call-done = f32[8,196]{1,0:T(8,128)} async-done(((f32[128,196]{1,0:T(8,128)}), f32[8,196]{1,0:T(8,128)}) %reduce-scatter.28.cloned.1.call-update) | async-done | bytes 6288
  923.1 58.4 %reduce-scatter.20.cloned.1.call-done = f32[4,128,8]{1,2,0:T(8,128)} async-done(((f32[4,128,128]{1,2,0:T(8,128)}), f32[4,128,8]{1,2,0:T(8,128)}) %reduce-scatter.20.cloned.1.call-update) | async-done | bytes 16400 | tf_op jit(solution)/shard_map/reduce_scatter | solution.py:304
  981.5 37.8 %reduce-scatter.16.cloned.1.call-done = bf16[1,208,1600]{2,1,0:T(8,128)(2,1)} async-done(((bf16[1,832,1600]{2,1,0:T(8,128)(2,1)}), bf16[1,208,1600]{2,1,0:T(8,128)(2,1)}) %reduce-scatter.16.cloned.1.call-update) | async-done | bytes 665616 | tf_op jit(solution)/shard_map/reduce_scatter | solution.py:296
  (456 shorter events, 377.7 us)
Async XLA Ops:
  7.2 197.3 %all-gather.6.cloned.1.call-start = ((), (), s32[]{:S(2)}) async-start(), calls=%async_computation.7 | async-start | bytes 2263040 | tf_op jit(solution)/shard_map/all_gather | solution.py:136
  7.9 713.1 %reduce-scatter.24.cloned.1.call-start = ((), (), s32[]{:S(2)}) async-start(), calls=%async_computation.12 | async-start | bytes 3584000
  89.9 6.6 collective-permute-start
  108.5 8.8 collective-permute-start
  129.4 7.9 collective-permute-start
  149.5 7.7 collective-permute-start
  158.9 18.1 %collective-permute-start = (f32[1,32,1600]{2,1,0:T(8,128)S(1)}, f32[1,32,1600]{2,1,0:T(8,128)S(1)}, u32[]{:S(2)}, u32[]{:S(2)}) collective-permute-start(f32[1,32,1600]{2,1,0:T(8,128)S(1)} %get-tuple-element.1329), channel_id=1, source_target_pairs={{0,4},{4,8},{8,12},{1,5},{5,9},{9,13},{2,6},{6,10},{10,14},{3,7},{... | collective-permute-start | bytes 614408 | tf_op jit(solution)/shard_map/while/body/eval_jaxpr/ppermute | solution.py:15
  178.8 7.7 collective-permute-start
  188.2 16.2 %collective-permute-start = (f32[1,32,1600]{2,1,0:T(8,128)S(1)}, f32[1,32,1600]{2,1,0:T(8,128)S(1)}, u32[]{:S(2)}, u32[]{:S(2)}) collective-permute-start(f32[1,32,1600]{2,1,0:T(8,128)S(1)} %get-tuple-element.1329), channel_id=1, source_target_pairs={{0,4},{4,8},{8,12},{1,5},{5,9},{9,13},{2,6},{6,10},{10,14},{3,7},{... | collective-permute-start | bytes 614408 | tf_op jit(solution)/shard_map/while/body/eval_jaxpr/ppermute | solution.py:15
  204.4 72.9 %copy-start.15 = (bf16[128,196]{1,0:T(8,128)(2,1)S(1)}, bf16[128,196]{1,0:T(8,128)(2,1)}, u32[]{:S(2)}) copy-start(bf16[128,196]{1,0:T(8,128)(2,1)} %all_gather.47) | copy-start | bytes 150532
  204.4 72.9 %copy-start.18 = (s32[4,1,384]{2,1,0:T(1,128)S(1)}, s32[4,1,384]{2,1,0:T(1,128)}, u32[]{:S(2)}) copy-start(s32[4,1,384]{2,1,0:T(1,128)} %param.23) | copy-start | bytes 18436
  204.4 72.9 %copy-start.19 = (s32[4,1,384]{2,1,0:T(1,128)S(1)}, s32[4,1,384]{2,1,0:T(1,128)}, u32[]{:S(2)}) copy-start(s32[4,1,384]{2,1,0:T(1,128)} %param.24) | copy-start | bytes 18436
  204.4 72.9 %copy-start.20 = (f32[4,1,384]{2,1,0:T(1,128)S(1)}, f32[4,1,384]{2,1,0:T(1,128)}, u32[]{:S(2)}) copy-start(f32[4,1,384]{2,1,0:T(1,128)} %param.25) | copy-start | bytes 18436
  347.5 6.4 copy-start.13
  351.5 7.1 copy-start.9
  361.8 6.8 collective-permute-start.1
  371.8 6.8 collective-permute-start.1
  381.8 94.9 %collective-permute-start.1 = (bf16[1,32,1600]{2,1,0:T(8,128)(2,1)}, bf16[1,32,1600]{2,1,0:T(8,128)(2,1)S(1)}, u32[]{:S(2)}, u32[]{:S(2)}) collective-permute-start(bf16[1,32,1600]{2,1,0:T(8,128)(2,1)} %get-tuple-element.1198), channel_id=1, source_target_pairs={{4,0},{8,4},{12,8},{5,1},{9,5},{13,9},{6,2},{10,6},{14,10},{7,3},{... | collective-permute-start | bytes 307208 | tf_op jit(solution)/shard_map/while/body/eval_jaxpr/ppermute | solution.py:15
  506.0 3.8 copy-start.7
  509.8 7.6 collective-permute-start.1
  550.5 7.6 collective-permute-start.1
  587.4 3.8 copy-start.7
  591.2 7.6 collective-permute-start.1
  628.1 3.8 copy-start.7
  631.9 7.0 collective-permute-start.1
  658.1 75.1 %reduce-scatter.26.cloned.1.call-start = ((), (), s32[]{:S(2)}) async-start(), calls=%async_computation.13 | async-start | bytes 3584000
  680.8 91.0 %reduce-scatter.22.cloned.1.call-start = ((), (), s32[]{:S(2)}) async-start(), calls=%async_computation.11 | async-start | bytes 3584000
  702.6 6.4 copy-start.12
  702.6 162.1 %reduce-scatter.18.cloned.1.call-start = ((), (), s32[]{:S(2)}) async-start(), calls=%async_computation.9 | async-start | bytes 7241728 | tf_op jit(solution)/shard_map/reduce_scatter | solution.py:301
  713.9 209.2 %reduce-scatter.28.cloned.1.call-start = ((), (), s32[]{:S(2)}) async-start(), calls=%async_computation.14 | async-start | bytes 139264
  715.7 265.8 %reduce-scatter.20.cloned.1.call-start = ((), (), s32[]{:S(2)}) async-start(), calls=%async_computation.10 | async-start | bytes 278528 | tf_op jit(solution)/shard_map/reduce_scatter | solution.py:304
  717.5 301.8 %reduce-scatter.16.cloned.1.call-start = ((), (), s32[]{:S(2)}) async-start(), calls=%async_computation.8 | async-start | bytes 3461120 | tf_op jit(solution)/shard_map/reduce_scatter | solution.py:296
  (33 other events, 87.2 us)
Sparse Core Ops, SparseCore 0:
  10.2 44.4 all-gather.5
  658.2 35.9 reduce-scatter.23
  696.9 36.2 reduce-scatter.25
  735.6 36.2 reduce-scatter.21
  776.2 88.4 reduce-scatter.17
  868.6 54.4 reduce-scatter.27
  927.2 54.2 reduce-scatter.19
  984.6 34.5 reduce-scatter.15
